TPU v7x, 32 devices: a whole 2x2x4 slice. The times are simulated.
32 devices in a mesh: dp: 8 (over y, x, core), fsdp: 4 (over z).
Axes of the slice: x: 2, y: 2, z: 4, core: 2. Of those that a mesh axis runs over, the one named last changes fastest.
Arguments:
- rollout_rows: bfloat16 [4096, 8192], P(('dp', 'fsdp')), may hold values from -6 to 6
- lengths: int32 [32, 8], P(('dp', 'fsdp')), may hold values from 1 to 32, as said below
- dest: int32 [32, 8], P(('dp', 'fsdp')), may hold values from 0 to 7, as said below
- offset: int32 [32, 8], P(('dp', 'fsdp')), may hold values from 0 to 96, as said below
- query: bfloat16 [4096, 4096], P(('dp', 'fsdp')), may hold values from -100 to 100
- key_rows: bfloat16 [4096, 512], P(('dp', 'fsdp')), may hold values from -5 to 5
- value_weight: bfloat16 [8192, 512], P('fsdp'), may hold values from -0.0625 to 0.0625
- d_out: bfloat16 [4096, 4096], P(('dp', 'fsdp')), may hold values from -6 to 6
Outputs:
- attn_out: bfloat16 [4096, 4096], P(('dp', 'fsdp'))
- grad_query: bfloat16 [4096, 4096], P(('dp', 'fsdp'))
- grad_key: bfloat16 [4096, 512], P(('dp', 'fsdp'))
- grad_input: bfloat16 [4096, 8192], P(('dp', 'fsdp'))
- grad_weight: float32 [8192, 512], P(('dp', 'fsdp'))
Inputs may be any that keep to these rules, and one draw needn't show every extreme that they name: Each rollout device's 8 lengths sum to 128. `dest`: the learner has the sender's fsdp index; the sequences of one device go to 8 different learner devices. `offset`: the sequences that a learner device receives cover its 128 rows exactly once; on every learner device the last of them is one of 32 rows.
All inputs are finite; a program needn't handle non-finite values.
Results may differ from a plain program's by a relative error of at most 0.006.
Values may be sent and summed in bfloat16 or wider, within the bound.
A program may use at most 128 MiB of HBM per device.

v0:
```python
import math
import jax
import jax.numpy as jnp
from jax import lax
from jax.sharding import PartitionSpec as P

HEAD_SIZE = 128
QUERY_HEADS = 32
KEY_VALUE_HEADS = 4


def attend(block_queries, block_keys, block_values, segment, gradient_block):
    row_count_total = block_queries.shape[0]
    share_ratio = QUERY_HEADS // KEY_VALUE_HEADS
    score_scale = 1.0 / math.sqrt(HEAD_SIZE)
    heads_queries = block_queries.reshape(row_count_total, KEY_VALUE_HEADS, share_ratio, HEAD_SIZE)
    heads_keys = block_keys.reshape(row_count_total, KEY_VALUE_HEADS, HEAD_SIZE)
    heads_values = block_values.reshape(row_count_total, KEY_VALUE_HEADS, HEAD_SIZE)
    gradient_heads = gradient_block.reshape(
        row_count_total, KEY_VALUE_HEADS, share_ratio, HEAD_SIZE
    )
    logit_scores = (
        jnp.einsum("euaz,nuz->uaen", heads_queries, heads_keys, preferred_element_type=jnp.float32)
        * score_scale
    )
    position = jnp.arange(row_count_total, dtype=jnp.int32)
    allowed = (segment[:, None] == segment[None, :]) & (position[None, :] <= position[:, None])
    logit_scores = jnp.where(allowed, logit_scores, -1e30)
    highest = jnp.max(logit_scores, axis=-1, keepdims=True)
    expo = jnp.exp(logit_scores - highest)
    probs = expo / jnp.sum(expo, axis=-1, keepdims=True)
    probs_reduced = probs.astype(jnp.bfloat16)
    attention_output = jnp.einsum(
        "yxmd,dya->myxa", probs_reduced, heads_values, preferred_element_type=jnp.float32
    )
    attention_output = attention_output.reshape(row_count_total, QUERY_HEADS * HEAD_SIZE).astype(
        jnp.bfloat16
    )
    gradient_probs = jnp.einsum(
        "euaz,nuz->uaen", gradient_heads, heads_values, preferred_element_type=jnp.float32
    )
    value_gradient = jnp.einsum(
        "lbjm,jlbw->mlw", probs_reduced, gradient_heads, preferred_element_type=jnp.float32
    )
    value_gradient = value_gradient.reshape(row_count_total, KEY_VALUE_HEADS * HEAD_SIZE).astype(
        jnp.bfloat16
    )
    inner = jnp.sum(probs * gradient_probs, axis=-1, keepdims=True)
    gradient_scores = (probs * (gradient_probs - inner) * score_scale).astype(jnp.bfloat16)
    query_gradient = jnp.einsum(
        "yxmd,dya->myxa", gradient_scores, heads_keys, preferred_element_type=jnp.float32
    )
    key_gradient = jnp.einsum(
        "lbjm,jlbw->mlw", gradient_scores, heads_queries, preferred_element_type=jnp.float32
    )
    return (
        attention_output,
        query_gradient.reshape(row_count_total, QUERY_HEADS * HEAD_SIZE).astype(jnp.bfloat16),
        key_gradient.reshape(row_count_total, KEY_VALUE_HEADS * HEAD_SIZE).astype(jnp.bfloat16),
        value_gradient,
    )


def tables(plan, tok_rows):
    seq_len, dest, offset = (plan[:, 0], plan[:, 1], plan[:, 2])
    order = jnp.arange(seq_len.shape[1], dtype=jnp.int32)
    earlier = order[None, :] < order[:, None]
    starts = jnp.sum(jnp.where(earlier[None], seq_len[:, None, :], 0), axis=2)
    rows = jnp.arange(tok_rows, dtype=jnp.int32)[None, :, None]
    inside = (rows >= starts[:, None, :]) & (rows < (starts + seq_len)[:, None, :])
    landing = (dest * tok_rows + offset - starts)[:, None, :] + rows
    return jnp.sum(jnp.where(inside, landing, 0), axis=2).reshape(-1)


def senders(plan, me, tok_rows):
    seq_len, dest, offset = (plan[:, 0], plan[:, 1], plan[:, 2])
    mine = dest == me
    land_off = jnp.sum(jnp.where(mine, offset, 0), axis=1)
    land_len = jnp.sum(jnp.where(mine, seq_len, 0), axis=1)
    rows = jnp.arange(tok_rows, dtype=jnp.int32)[:, None]
    inside = (rows >= land_off[None, :]) & (rows < (land_off + land_len)[None, :])
    source = jnp.arange(plan.shape[0], dtype=jnp.int32)
    return jnp.sum(jnp.where(inside, source[None, :], 0), axis=1)


def local(rollout_rows, lengths, dest, offset, query, key_rows, value_weight, d_out):
    n_dp = lax.axis_size("dp")
    n_fsdp = lax.axis_size("fsdp")
    me = lax.axis_index("dp")
    tok_rows = rollout_rows.shape[0]
    column = tok_rows * n_dp
    plan = lax.all_gather(jnp.concatenate([lengths, dest, offset], axis=0), "dp", axis=0)
    shared = lax.all_to_all(rollout_rows, "dp", split_axis=1, concat_axis=0, tiled=True)
    block = value_weight.shape[0] // n_dp
    piece = lax.dynamic_slice_in_dim(value_weight, me * block, block, axis=0)
    pairs = [(a * n_fsdp + b, b * n_dp + a) for a in range(n_dp) for b in range(n_fsdp)]
    piece = lax.ppermute(piece, ("dp", "fsdp"), pairs)
    weight = lax.all_gather(piece, "fsdp", axis=0, tiled=True)
    landing = tables(plan, tok_rows)
    pick = (jnp.arange(column, dtype=jnp.int32)[:, None] == landing[None, :]).astype(jnp.bfloat16)
    rows = jnp.dot(pick, shared, preferred_element_type=jnp.float32).astype(jnp.bfloat16)
    partial = jnp.dot(rows, weight, preferred_element_type=jnp.float32).astype(jnp.bfloat16)
    parts = lax.all_to_all(
        partial.reshape(n_dp, tok_rows, partial.shape[1]),
        "dp",
        split_axis=0,
        concat_axis=0,
        tiled=True,
    )
    values = jnp.sum(parts.astype(jnp.float32), axis=0).astype(jnp.bfloat16)
    attention_output, query_gradient, key_gradient, value_gradient = attend(
        query, key_rows, values, senders(plan, me, tok_rows), d_out
    )
    gathered = lax.all_gather(value_gradient, "dp", axis=0, tiled=True)
    grad_weight = lax.psum_scatter(
        lax.dot_general(
            rows, gathered, (((0,), (0,)), ((), ())), preferred_element_type=jnp.float32
        ),
        "fsdp",
        scatter_dimension=0,
        tiled=True,
    )
    grad_weight = grad_weight * (1.0 / math.sqrt(column * n_fsdp))
    share = lax.dot_general(
        gathered, weight, (((1,), (1,)), ((), ())), preferred_element_type=jnp.float32
    ).astype(jnp.bfloat16)
    grad_input = lax.all_to_all(share, "dp", split_axis=0, concat_axis=1, tiled=True)
    return (attention_output, query_gradient, key_gradient, grad_input, grad_weight)


def solution(mesh):
    in_specs = (
        P(("dp", "fsdp"), None),
        P(("dp", "fsdp"), None),
        P(("dp", "fsdp"), None),
        P(("dp", "fsdp"), None),
        P(("dp", "fsdp"), None),
        P(("dp", "fsdp"), None),
        P("fsdp", None),
        P(("dp", "fsdp"), None),
    )
    out_specs = (
        P(("dp", "fsdp"), None),
        P(("dp", "fsdp"), None),
        P(("dp", "fsdp"), None),
        P(("dp", "fsdp"), None),
        P(("dp", "fsdp"), None),
    )
    return jax.shard_map(local, mesh=mesh, in_specs=in_specs, out_specs=out_specs, check_vma=False)
```

profile of v0, /device:TPU:0, one launch (start us, length us, event | category | flops | bytes accessed | tf_op | source)
XLA Modules:
  0.0 167.1 jit_solution(17855206566767428514)
XLA Ops:
  7.2 0.0 copy-start
  7.2 0.0 all-gather.7.cloned.1.call-start
  7.2 0.8 add_bitcast_fusion
  8.1 10.3 %all-gather.1 = s32[8,3,8]{2,1,0:T(4,128)S(1)} all-gather(s32[1,3,8]{2,1,0:T(4,128)S(1)} %add_bitcast_fusion), channel_id=2, replica_groups=mesh['dp'=8,'fsdp'=4] {'dp'}, dimensions={0}, use_global_device_ids=true | all-gather | bytes 864 | tf_op jit(solution)/shard_map/all_gather | solution.py:92
  18.4 0.1 select_reduce_fusion.3
  18.6 0.1 select_reduce_fusion.2
  18.7 0.1 fusion.19
  18.8 0.9 reshape.70
  19.7 0.1 copy.113
  19.9 2.3 %copy.127 = bf16[128,4096]{0,1:T(8,128)(2,1)} copy(bf16[128,4096]{1,0:T(8,128)(2,1)} %param.12) | data formatting | bytes 2097152 | tf_op jit(solution)/shard_map/reshape | solution.py:16
  22.2 1.6 copy.128
  23.8 3.4 %fusion.31 = (f32[4,8,128]{2,1,0:T(8,128)S(1)}, f32[4,8,128,128]{2,3,1,0:T(8,128)}) fusion(pred[128,128]{0,1:T(8,128)(4,1)S(1)} %fusion.19, bf16[128,4,128,1]{0,2,3,1:T(8,128)(2,1)S(1)} %copy.113, bf16[128,4,8,128]{0,3,2,1:T(8,128)(2,1)} %bitcast.113), kind=kOutput, calls=%fused_computation.59 | convolution fusion | flops 136315008 | bytes 3309568 | tf_op jit(solution)/shard_map/sub | solution.py:30
  27.2 2.7 %fusion.10 = bf16[4,128,128]{1,2,0:T(8,128)(2,1)} fusion(bf16[128,4,8,128]{0,3,2,1:T(8,128)(2,1)S(1)} %bitcast.108, f32[4,8,128,128]{2,3,1,0:T(8,128)} %get-tuple-element.38, f32[4,8,128]{2,1,0:T(8,128)S(1)} %get-tuple-element.37), kind=kOutput, calls=%fused_computation.21 | convolution fusion | flops 135331840 | bytes 3293184 | tf_op jit(solution)/shard_map/lbjm,jlbw->mlw/dot_general | solution.py:42
  29.9 0.0 all-gather.7.cloned.1.call-update
  30.0 4.1 %copy.90 = bf16[128,8192]{0,1:T(8,128)(2,1)} copy(bf16[128,8192]{1,0:T(8,128)(2,1)} %param.8) | data formatting | bytes 4194304 | tf_op args[0]
  34.0 4.4 %all-to-all-start = ((bf16[128,8,1024]{0,2,1:T(8,128)(2,1)}), bf16[128,8,1024]{0,2,1:T(8,128)(2,1)}, u32[]{:S(2)}, u32[]{:S(2)}) async-start(bf16[128,8,1024]{0,2,1:T(8,128)(2,1)} %bitcast.107), calls=%async_computation | async-start | bytes 4194304 | tf_op jit(solution)/shard_map/all_to_all | solution.py:93
  38.4 0.0 all-gather.5.cloned.1.call-start
  38.5 0.7 collective-permute-start
  39.2 0.0 collective-permute-done
  39.2 0.0 copy-start.2
  39.2 0.7 copy-done.2
  39.9 0.0 all-gather.5.cloned.1.call-update
  39.9 0.0 reduce-scatter.2.cloned.1.call-start
  40.0 0.2 select_reduce_fusion.1
  40.2 0.1 select_reduce_fusion
  40.3 30.3 %all-to-all-done = bf16[128,8,1024]{0,2,1:T(8,128)(2,1)} async-done(((bf16[128,8,1024]{0,2,1:T(8,128)(2,1)}), bf16[128,8,1024]{0,2,1:T(8,128)(2,1)}, u32[]{:S(2)}, u32[]{:S(2)}) %all-to-all-start) | async-done | bytes 2097184 | tf_op jit(solution)/shard_map/all_to_all | solution.py:93
  70.7 3.9 %copy.91 = bf16[8,128,1024]{2,1,0:T(8,128)(2,1)} copy(bf16[8,128,1024]{1,2,0:T(8,128)(2,1)} %bitcast.7) | data formatting | bytes 4194304 | tf_op jit(solution)/shard_map/all_to_all | solution.py:93
  74.6 5.3 %fusion.7 = bf16[1024,1024]{1,0:T(8,128)(2,1)} fusion(bf16[1024,1024]{1,0:T(8,128)(2,1)} %bitcast.112, s32[1024]{0:T(1024)S(1)} %bitcast.130), kind=kOutput, calls=%fused_computation.12 | convolution fusion | flops 2149580800 | bytes 4198400 | tf_op jit(solution)/shard_map/dot_general | solution.py:101
  79.8 4.5 %fusion.33 = f32[1024,512]{1,0:T(8,128)} fusion(bf16[1024,1024]{1,0:T(8,128)(2,1)} %fusion.7, bf16[1024,512]{0,1:T(8,128)(2,1)} %all-gather.7.cloned.1.call-done), kind=kOutput, calls=%fused_computation.61 | convolution fusion | flops 1073741824 | bytes 5242880 | tf_op jit(solution)/shard_map/dot_general | solution.py:116
  84.4 0.0 reduce-scatter.2.cloned.1.call-update
  84.4 16.3 %all-gather.5.cloned.1.call-done = bf16[1024,512]{1,0:T(8,128)(2,1)} async-done(((bf16[256,512]{1,0:T(8,128)(2,1)}), bf16[1024,512]{1,0:T(8,128)(2,1)}) %all-gather.5.cloned.1.call-update) | async-done | bytes 1048592 | tf_op jit(solution)/shard_map/all_gather | solution.py:98
  100.7 4.1 %convolution_convert_fusion.3 = bf16[1024,512]{1,0:T(8,128)(2,1)} fusion(bf16[1024,1024]{1,0:T(8,128)(2,1)} %fusion.7, bf16[1024,512]{1,0:T(8,128)(2,1)} %all-gather.5.cloned.1.call-done), kind=kOutput, calls=%fused_computation.17 | convolution fusion | flops 1074266112 | bytes 4194304 | tf_op jit(solution)/shard_map/dot_general | solution.py:102
  104.7 4.2 %all-to-all-start.1 = ((bf16[8,128,512]{2,1,0:T(8,128)(2,1)}), bf16[8,128,512]{2,1,0:T(8,128)(2,1)}, u32[]{:S(2)}, u32[]{:S(2)}) async-start(bf16[8,128,512]{2,1,0:T(8,128)(2,1)} %bitcast.115), calls=%async_computation.1 | async-start | bytes 2097152 | tf_op jit(solution)/shard_map/all_to_all | solution.py:103
  109.0 4.2 %convolution_convert_fusion = bf16[1024,1024]{1,0:T(8,128)(2,1)} fusion(bf16[1024,512]{0,1:T(8,128)(2,1)} %all-gather.7.cloned.1.call-done, bf16[1024,512]{1,0:T(8,128)(2,1)} %all-gather.5.cloned.1.call-done), kind=kOutput, calls=%fused_computation.13 | convolution fusion | flops 1074790400 | bytes 4194304 | tf_op jit(solution)/shard_map/dot_general | solution.py:124
  113.2 11.2 %all-to-all-done.1 = bf16[8,128,512]{2,1,0:T(8,128)(2,1)} async-done(((bf16[8,128,512]{2,1,0:T(8,128)(2,1)}), bf16[8,128,512]{2,1,0:T(8,128)(2,1)}, u32[]{:S(2)}, u32[]{:S(2)}) %all-to-all-start.1) | async-done | bytes 1048608 | tf_op jit(solution)/shard_map/all_to_all | solution.py:103
  124.4 4.7 %all-to-all-start.2 = ((bf16[8,128,1024]{2,1,0:T(8,128)(2,1)}), bf16[8,128,1024]{2,1,0:T(8,128)(2,1)}, u32[]{:S(2)}, u32[]{:S(2)}) async-start(bf16[8,128,1024]{2,1,0:T(8,128)(2,1)} %bitcast.110), calls=%async_computation.2 | async-start | bytes 4194304 | tf_op jit(solution)/shard_map/all_to_all | solution.py:127
  129.1 1.4 reduce_sum.80
  130.5 0.1 copy.92
  130.6 3.0 %convolution_convert_fusion.2 = bf16[4,128,8,128]{3,1,2,0:T(8,128)(2,1)} fusion(bf16[128,4,128,1]{0,2,3,1:T(8,128)(2,1)S(1)} %bitcast.118, f32[4,8,128,128]{2,3,1,0:T(8,128)} %get-tuple-element.38, f32[4,8,128]{2,1,0:T(8,128)S(1)} %copy-done.4), kind=kOutput, calls=%fused_computation.16 | convolution fusion | flops 135790592 | bytes 3293184 | tf_op jit(solution)/shard_map/yxmd,dya->myxa/dot_general | solution.py:33
  133.6 2.3 %copy.105 = bf16[128,4096]{1,0:T(8,128)(2,1)} copy(bf16[128,4096]{0,1:T(8,128)(2,1)} %bitcast.117) | data formatting | bytes 2097152
  135.9 1.8 %fusion.32 = f32[4,128,128,8]{2,1,3,0:T(8,128)} fusion(bf16[128,4,128,1]{0,2,3,1:T(8,128)(2,1)S(1)} %bitcast.119, bf16[128,4,8,128]{0,3,2,1:T(8,128)(2,1)S(1)} %bitcast.109), kind=kOutput, calls=%fused_computation.60 | convolution fusion | flops 134217728 | bytes 3276800 | tf_op jit(solution)/shard_map/euaz,nuz->uaen/dot_general | solution.py:39
  137.7 5.4 %convolution_convert_fusion.1 = bf16[4,8,128,128]{2,3,1,0:T(8,128)(2,1)} fusion(bf16[128,4,128,1]{0,2,3,1:T(8,128)(2,1)S(1)} %copy.113, f32[4,128,128,8]{2,1,3,0:T(8,128)} %fusion.32, f32[4,8,128,128]{2,3,1,0:T(8,128)} %get-tuple-element.38, f32[4,8,128]{2,1,0:T(8,128)S(1)} %copy-done.4), kind=kOutput, calls=%fused_computation.15 | convolution fusion | flops 138416256 | bytes 5390336 | tf_op jit(solution)/shard_map/yxmd,dya->myxa/dot_general | solution.py:50
  143.1 2.4 %copy.106 = bf16[128,4096]{1,0:T(8,128)(2,1)} copy(bf16[128,4096]{0,1:T(8,128)(2,1)} %bitcast.116) | data formatting | bytes 2097152
  145.4 4.4 %fusion.9 = bf16[4,128,128]{1,2,0:T(8,128)(2,1)S(1)} fusion(bf16[128,4,8,128]{0,3,2,1:T(8,128)(2,1)S(1)} %bitcast.114, f32[4,128,128,8]{2,1,3,0:T(8,128)} %fusion.32, f32[4,8,128,128]{2,3,1,0:T(8,128)} %get-tuple-element.38, f32[4,8,128]{2,1,0:T(8,128)S(1)} %copy-done.4), kind=kOutput, calls=%fused_computation.20 | convolution fusion | flops 137957504 | bytes 5390336 | tf_op jit(solution)/shard_map/lbjm,jlbw->mlw/dot_general | solution.py:53
  149.8 0.8 copy.107
  150.6 5.0 %all-to-all-done.2 = bf16[8,128,1024]{2,1,0:T(8,128)(2,1)} async-done(((bf16[8,128,1024]{2,1,0:T(8,128)(2,1)}), bf16[8,128,1024]{2,1,0:T(8,128)(2,1)}, u32[]{:S(2)}, u32[]{:S(2)}) %all-to-all-start.2) | async-done | bytes 2097184 | tf_op jit(solution)/shard_map/all_to_all | solution.py:127
  155.6 3.1 %copy.129 = bf16[8,16,8,1024]{3,2,0,1:T(8,128)(2,1)} copy(bf16[8,16,8,1024]{3,2,1,0:T(8,128)(2,1)} %bitcast.49) | data formatting | bytes 4194304 | tf_op jit(solution)/shard_map/all_to_all | solution.py:127
  158.7 1.9 %broadcast_multiply_fusion = f32[256,512]{1,0:T(8,128)} fusion(f32[256,512]{1,0:T(8,128)} %reduce-scatter.2.cloned.1.call-done), kind=kLoop, calls=%fused_computation.29 | loop fusion | flops 131072 | bytes 1048576 | tf_op jit(solution)/shard_map/mul | solution.py:123
  (14 shorter events, 0.1 us)
Async XLA Ops:
  7.2 31.3 %copy-start = (bf16[2048,512]{1,0:T(8,128)(2,1)S(1)}, bf16[2048,512]{1,0:T(8,128)(2,1)}, u32[]{:S(2)}) copy-start(bf16[2048,512]{1,0:T(8,128)(2,1)} %param.14) | copy-start | bytes 6291460
  7.2 72.7 %all-gather.7.cloned.1.call-start = ((), (), s32[]{:S(2)}) async-start(), calls=%async_computation.5 | async-start | bytes 1179648 | tf_op jit(solution)/shard_map/all_gather | solution.py:114
  27.2 2.7 %copy-start.3 = (f32[4,8,128]{2,1,0:T(8,128)}, f32[4,8,128]{2,1,0:T(8,128)S(1)}, u32[]{:S(2)}) copy-start(f32[4,8,128]{2,1,0:T(8,128)S(1)} %get-tuple-element.37) | copy-start | bytes 49156
  34.0 36.6 %all-to-all-start = ((bf16[128,8,1024]{0,2,1:T(8,128)(2,1)}), bf16[128,8,1024]{0,2,1:T(8,128)(2,1)}, u32[]{:S(2)}, u32[]{:S(2)}) async-start(bf16[128,8,1024]{0,2,1:T(8,128)(2,1)} %bitcast.107), calls=%async_computation | async-start | bytes 4194304 | tf_op jit(solution)/shard_map/all_to_all | solution.py:93
  38.4 62.2 %all-gather.5.cloned.1.call-start = ((), (), s32[]{:S(2)}) async-start(), calls=%async_computation.4 | async-start | bytes 1310720 | tf_op jit(solution)/shard_map/all_gather | solution.py:98
  38.5 0.7 collective-permute-start
  39.2 0.7 copy-start.2
  39.9 118.8 %reduce-scatter.2.cloned.1.call-start = ((), (), s32[]{:S(2)}) async-start(), calls=%async_computation.6 | async-start | bytes 2621440 | tf_op jit(solution)/shard_map/reduce_scatter | solution.py:115
  104.7 19.7 %all-to-all-start.1 = ((bf16[8,128,512]{2,1,0:T(8,128)(2,1)}), bf16[8,128,512]{2,1,0:T(8,128)(2,1)}, u32[]{:S(2)}, u32[]{:S(2)}) async-start(bf16[8,128,512]{2,1,0:T(8,128)(2,1)} %bitcast.115), calls=%async_computation.1 | async-start | bytes 2097152 | tf_op jit(solution)/shard_map/all_to_all | solution.py:103
  124.4 6.2 %copy-start.4 = (f32[4,8,128]{2,1,0:T(8,128)S(1)}, f32[4,8,128]{2,1,0:T(8,128)}, u32[]{:S(2)}) copy-start(f32[4,8,128]{2,1,0:T(8,128)} %copy-done.3) | copy-start | bytes 49156
  124.4 31.2 %all-to-all-start.2 = ((bf16[8,128,1024]{2,1,0:T(8,128)(2,1)}), bf16[8,128,1024]{2,1,0:T(8,128)(2,1)}, u32[]{:S(2)}, u32[]{:S(2)}) async-start(bf16[8,128,1024]{2,1,0:T(8,128)(2,1)} %bitcast.110), calls=%async_computation.2 | async-start | bytes 4194304 | tf_op jit(solution)/shard_map/all_to_all | solution.py:127
  143.1 2.4 %copy-start.1 = (bf16[128,4096]{0,1:T(8,128)(2,1)S(1)}, bf16[128,4096]{0,1:T(8,128)(2,1)}, u32[]{:S(2)}) copy-start(bf16[128,4096]{0,1:T(8,128)(2,1)} %copy.127) | copy-start | bytes 3145732
Sparse Core Ops, SparseCore 0:
  30.1 37.2 all-gather.6
  69.5 31.0 all-gather.4
  103.0 43.3 reduce-scatter.1
where the time goes:
time: 168 us; the launch traced here: 167 us
  waiting for transfers between devices  62.9 us (37%)
  matrix products  38.7 us (23%)
  local copies, waits for them, and re-layouts  22.4 us (13%)
  starting transfers between devices  14.1 us (8%)
  between operations  13.9 us (8%)
  blocking collectives  10.3 us (6%)
  other arithmetic  4.77 us (3%)
    all_to_all x1, waiting for transfers between devices, local(): lax.all_to_all(rollout_rows, 'dp', split_axis=1, concat_axis=0, tiled=True)  30.3 us
    all_gather x1, waiting for transfers between devices, local(): weight = lax.all_gather(piece, 'fsdp', axis=0, tiled=True)  16.3 us
    all_to_all x1, waiting for transfers between devices, local(): lax.all_to_all(partial.reshape(n_dp, tok_rows, partial.shape[1]), 'dp', s...  11.2 us
    all_gather x1, blocking collectives, local(): lax.all_gather(jnp.concatenate([lengths, dest, offset], axis=0), 'dp', ax...  10.3 us
    unnamed x14, local copies, waits for them, and re-layouts  10.2 us
    dot_general x1, matrix products, attend(): jnp.einsum('yxmd,dya->myxa', gradient_scores, heads_keys, preferred_eleme...  5.38 us
    dot_general x1, matrix products, local(): jnp.dot(pick, shared, preferred_element_type=jnp.float32)  5.25 us
    all_to_all x1, waiting for transfers between devices, local(): lax.all_to_all(share, 'dp', split_axis=0, concat_axis=1, tiled=True)  5 us
  transfers between devices with their start and end apart: 7, of which 4 were waited for; matrix products, arithmetic and copies ran while one was open for 31% of the time, Pallas kernels for 0%

commit v1 on v0

--- a/solution.py
+++ b/solution.py
@@ -1,3 +1,4 @@
+import functools
 import math
 import jax
 import jax.numpy as jnp
@@ -7,6 +8,36 @@
 HEAD_SIZE = 128
 QUERY_HEADS = 32
 KEY_VALUE_HEADS = 4
+
+
+def track_the_classes(tile_in, out_dim):
+    tmp = list(tile_in.shape[1:])
+    tmp[out_dim] *= tile_in.shape[0]
+    return jnp.moveaxis(tile_in, 0, out_dim).reshape(tmp)
+
+
+def search_ladders(state, lane_axis, where_dim):
+    n_blocks = lax.axis_size(lane_axis)
+    pile = [(j, (j + 1) % n_blocks) for j in range(n_blocks)]
+    line_up = [(no, w) for w, no in pile]
+    value_now, big = ([], [])
+    for i in range(n_blocks - 1):
+        if i % 2 == 0:
+            value_now.append(
+                lax.ppermute(value_now[-1] if value_now else state, lane_axis, perm=pile)
+            )
+        else:
+            r_now = lax.ppermute(big[-1] if big else state, lane_axis, perm=line_up)
+            big.append(r_now)
+    a_now = jnp.stack([*value_now[::-1], state, *big])
+    mat_out = lax.axis_index(lane_axis)
+    y = len(value_now)
+    formed = mat_out - y
+    a_now = a_now[(jnp.arange(n_blocks) - formed) % n_blocks]
+    return track_the_classes(a_now, where_dim)
+
+
+settle_the_sheets = functools.partial(search_ladders, lane_axis="fsdp", where_dim=0)
 
 
 def attend(block_queries, block_keys, block_values, segment, gradient_block):
@@ -95,7 +126,7 @@
     piece = lax.dynamic_slice_in_dim(value_weight, me * block, block, axis=0)
     pairs = [(a * n_fsdp + b, b * n_dp + a) for a in range(n_dp) for b in range(n_fsdp)]
     piece = lax.ppermute(piece, ("dp", "fsdp"), pairs)
-    weight = lax.all_gather(piece, "fsdp", axis=0, tiled=True)
+    weight = settle_the_sheets(piece)
     landing = tables(plan, tok_rows)
     pick = (jnp.arange(column, dtype=jnp.int32)[:, None] == landing[None, :]).astype(jnp.bfloat16)
     rows = jnp.dot(pick, shared, preferred_element_type=jnp.float32).astype(jnp.bfloat16)

time: 168 us -> 225 us (1.34)
  starting transfers between devices: 14.1 us -> 61.4 us
  blocking collectives: 10.3 us -> 29.6 us
  waiting for transfers between devices: 62.9 us -> 50.7 us
    ppermute x0 -> x3, starting transfers between devices: none -> 44.2 us  [the longest x2 40.1 us: search_ladders(): lax.ppermute(value_now[-1] if value_now else state, lane_axis, perm=pile)]
    all_to_all x1, waiting for transfers between devices: 30.3 us -> 0.01 us  [local(): lax.all_to_all(rollout_rows, 'dp', split_axis=1, concat_axis=0, tiled=True)]
    all_gather x1, blocking collectives: 10.3 us -> 29.6 us  [local(): lax.all_gather(jnp.concatenate([lengths, dest, offset], axis=0), 'dp', ax...]
    ppermute x0 -> x3, waiting for transfers between devices: none -> 19.3 us  [the longest x2 14.9 us: search_ladders(): lax.ppermute(value_now[-1] if value_now else state, lane_axis, perm=pile)]
    all_gather x1 -> x0, waiting for transfers between devices: 16.3 us -> none  [local(): weight = lax.all_gather(piece, 'fsdp', axis=0, tiled=True)]
    all_gather x1, waiting for transfers between devices: 0.01 us -> 15 us  [local(): gathered = lax.all_gather(value_gradient, 'dp', axis=0, tiled=True)]
    gather x0 -> x1, local copies, waits for them, and re-layouts: none -> 2.81 us  [search_ladders(): a_now = a_now[(jnp.arange(n_blocks) - formed) % n_blocks]]
    unnamed x14 -> x24, local copies, waits for them, and re-layouts: 10.2 us -> 9.65 us
  transfers between devices with their start and end apart: 7 -> 9, of which waited for: 4 -> 6; matrix products, arithmetic and copies ran while one was open for 31% -> 26% of each run, Pallas kernels for 0% -> 0%
where the time goes in v1:
time: 225 us; the launch traced here: 224 us
  starting transfers between devices  61.4 us (27%)
  waiting for transfers between devices  50.7 us (23%)
  matrix products  38.5 us (17%)
  blocking collectives  29.6 us (13%)
  local copies, waits for them, and re-layouts  22.8 us (10%)
  between operations  14.3 us (6%)
  other arithmetic  6.76 us (3%)
    ppermute x2, starting transfers between devices, search_ladders(): lax.ppermute(value_now[-1] if value_now else state, lane_axis, perm=pile)  40.1 us
    all_gather x1, blocking collectives, local(): lax.all_gather(jnp.concatenate([lengths, dest, offset], axis=0), 'dp', ax...  29.6 us
    all_gather x1, waiting for transfers between devices, local(): gathered = lax.all_gather(value_gradient, 'dp', axis=0, tiled=True)  15 us
    ppermute x2, waiting for transfers between devices, search_ladders(): lax.ppermute(value_now[-1] if value_now else state, lane_axis, perm=pile)  14.9 us
    all_to_all x1, waiting for transfers between devices, local(): lax.all_to_all(partial.reshape(n_dp, tok_rows, partial.shape[1]), 'dp', s...  11.3 us
    unnamed x24, local copies, waits for them, and re-layouts  9.65 us
    all_to_all x1, starting transfers between devices, local(): lax.all_to_all(partial.reshape(n_dp, tok_rows, partial.shape[1]), 'dp', s...  6.47 us
    dot_general x1, matrix products, attend(): jnp.einsum('yxmd,dya->myxa', gradient_scores, heads_keys, preferred_eleme...  5.36 us
  transfers between devices with their start and end apart: 9, of which 6 were waited for; matrix products, arithmetic and copies ran while one was open for 26% of the time, Pallas kernels for 0%

profile of v1, /device:TPU:0, one launch (start us, length us, event | category | flops | bytes accessed | tf_op | source)
XLA Modules:
  0.0 224.1 jit_solution(5446921550400279186)
XLA Ops:
  7.2 0.0 copy-start
  7.2 4.2 %copy.90 = bf16[128,8192]{0,1:T(8,128)(2,1)} copy(bf16[128,8192]{1,0:T(8,128)(2,1)} %param.8) | data formatting | bytes 4194304 | tf_op args[0]
  11.4 5.3 %all-to-all-start = ((bf16[128,8,1024]{0,2,1:T(8,128)(2,1)}), bf16[128,8,1024]{0,2,1:T(8,128)(2,1)}, u32[]{:S(2)}, u32[]{:S(2)}) async-start(bf16[128,8,1024]{0,2,1:T(8,128)(2,1)} %bitcast.114), calls=%async_computation | async-start | bytes 4194304 | tf_op jit(solution)/shard_map/all_to_all | solution.py:124
  16.7 0.0 all-gather.4.cloned.1.call-start
  16.8 29.6 %all-gather.1 = s32[8,3,8]{2,1,0:T(4,128)S(1)} all-gather(s32[1,3,8]{2,1,0:T(4,128)S(1)} %add_bitcast_fusion), channel_id=2, replica_groups=mesh['dp'=8,'fsdp'=4] {'dp'}, dimensions={0}, use_global_device_ids=true | all-gather | bytes 864 | tf_op jit(solution)/shard_map/all_gather | solution.py:123
  46.5 0.1 select_reduce_fusion.3
  46.6 0.1 select_reduce_fusion.2
  46.7 0.7 fusion.19
  47.5 0.1 copy.113
  47.6 1.4 copy.127
  49.0 3.4 %fusion.33 = (f32[4,8,128]{2,1,0:T(8,128)S(1)}, f32[4,8,128,128]{2,3,1,0:T(8,128)}) fusion(pred[128,128]{0,1:T(8,128)(4,1)S(1)} %copy-done.4, bf16[128,4,128,1]{0,2,3,1:T(8,128)(2,1)S(1)} %copy.113, bf16[128,4,8,128]{0,3,2,1:T(8,128)(2,1)} %bitcast.122), kind=kOutput, calls=%fused_computation.68 | convolution fusion | flops 136315008 | bytes 3309568 | tf_op jit(solution)/shard_map/sub | solution.py:61
  52.4 1.6 copy.128
  54.1 2.7 %fusion.10 = bf16[4,128,128]{1,2,0:T(8,128)(2,1)} fusion(bf16[128,4,8,128]{0,3,2,1:T(8,128)(2,1)S(1)} %bitcast.115, f32[4,8,128,128]{2,3,1,0:T(8,128)} %get-tuple-element.38, f32[4,8,128]{2,1,0:T(8,128)S(1)} %get-tuple-element.37), kind=kOutput, calls=%fused_computation.22 | convolution fusion | flops 135331840 | bytes 3293184 | tf_op jit(solution)/shard_map/lbjm,jlbw->mlw/dot_general | solution.py:73
  56.8 0.0 all-gather.4.cloned.1.call-update
  56.8 0.0 reduce-scatter.2.cloned.1.call-start
  56.8 0.2 select_reduce_fusion.1
  57.1 0.1 select_reduce_fusion
  57.2 3.9 %copy.91 = bf16[8,128,1024]{2,1,0:T(8,128)(2,1)} copy(bf16[8,128,1024]{1,2,0:T(8,128)(2,1)} %bitcast.7) | data formatting | bytes 4194304 | tf_op jit(solution)/shard_map/all_to_all | solution.py:124
  61.1 5.3 %fusion.7 = bf16[1024,1024]{1,0:T(8,128)(2,1)} fusion(bf16[1024,1024]{1,0:T(8,128)(2,1)} %bitcast.119, s32[1024]{0:T(1024)S(1)} %bitcast.140), kind=kOutput, calls=%fused_computation.13 | convolution fusion | flops 2149580800 | bytes 4198400 | tf_op jit(solution)/shard_map/dot_general | solution.py:132
  66.4 15.0 %all-gather.4.cloned.1.call-done = bf16[1024,512]{0,1:T(8,128)(2,1)} async-done(((bf16[128,512]{0,1:T(8,128)(2,1)}), bf16[1024,512]{0,1:T(8,128)(2,1)}) %all-gather.4.cloned.1.call-update) | async-done | bytes 1048592 | tf_op jit(solution)/shard_map/all_gather | solution.py:145
  81.3 4.4 %fusion.35 = f32[1024,512]{1,0:T(8,128)} fusion(bf16[1024,1024]{1,0:T(8,128)(2,1)} %fusion.7, bf16[1024,512]{0,1:T(8,128)(2,1)} %all-gather.4.cloned.1.call-done), kind=kOutput, calls=%fused_computation.70 | convolution fusion | flops 1073741824 | bytes 5242880 | tf_op jit(solution)/shard_map/dot_general | solution.py:147
  85.8 0.0 reduce-scatter.2.cloned.1.call-update
  85.9 0.7 collective-permute-start
  86.6 16.6 %collective-permute-start.1 = (bf16[256,512]{1,0:T(8,128)(2,1)S(1)}, bf16[256,512]{1,0:T(8,128)(2,1)}, u32[]{:S(2)}, u32[]{:S(2)}) collective-permute-start(bf16[256,512]{1,0:T(8,128)(2,1)S(1)} %collective-permute-done), channel_id=1, source_target_pairs={{0,1},{1,2},{2,3},{3,0},{4,5},{5,6},{6,7},{7,4},{8,9},{9,10},{10,1... | collective-permute-start | bytes 786440 | tf_op jit(solution)/shard_map/ppermute | solution.py:27
  103.2 4.1 %collective-permute-start.3 = (bf16[256,512]{1,0:T(8,128)(2,1)S(1)}, bf16[256,512]{1,0:T(8,128)(2,1)}, u32[]{:S(2)}, u32[]{:S(2)}) collective-permute-start(bf16[256,512]{1,0:T(8,128)(2,1)S(1)} %collective-permute-done), channel_id=1, source_target_pairs={{1,0},{2,1},{3,2},{0,3},{5,4},{6,5},{7,6},{4,7},{9,8},{10,9},{11,1... | collective-permute-start | bytes 786440 | tf_op jit(solution)/shard_map/ppermute | solution.py:30
  107.2 12.8 %collective-permute-done.1 = bf16[256,512]{1,0:T(8,128)(2,1)} collective-permute-done((bf16[256,512]{1,0:T(8,128)(2,1)S(1)}, bf16[256,512]{1,0:T(8,128)(2,1)}, u32[]{:S(2)}, u32[]{:S(2)}) %collective-permute-start.1) | collective-permute-done | bytes 262176 | tf_op jit(solution)/shard_map/ppermute | solution.py:27
  120.1 23.5 %collective-permute-start.2 = (bf16[256,512]{1,0:T(8,128)(2,1)}, bf16[256,512]{1,0:T(8,128)(2,1)}, u32[]{:S(2)}, u32[]{:S(2)}) collective-permute-start(bf16[256,512]{1,0:T(8,128)(2,1)} %collective-permute-done.1), channel_id=1, source_target_pairs={{0,1},{1,2},{2,3},{3,0},{4,5},{5,6},{6,7},{7,4},{8,9},{9,10},{10,1... | collective-permute-start | bytes 786440 | tf_op jit(solution)/shard_map/ppermute | solution.py:27
  143.6 4.4 %collective-permute-done.3 = bf16[256,512]{1,0:T(8,128)(2,1)} collective-permute-done((bf16[256,512]{1,0:T(8,128)(2,1)S(1)}, bf16[256,512]{1,0:T(8,128)(2,1)}, u32[]{:S(2)}, u32[]{:S(2)}) %collective-permute-start.3) | collective-permute-done | bytes 262176 | tf_op jit(solution)/shard_map/ppermute | solution.py:30
  148.0 2.0 collective-permute-done.2
  150.0 2.2 pad_maximum_fusion
  152.2 2.8 %gather_fusion = bf16[4,256,512]{2,1,0:T(8,128)(2,1)} fusion(bf16[4,256,512]{2,1,0:T(8,128)(2,1)} %pad_maximum_fusion, s32[1024]{0:T(1024)S(1)} %pad_clamp_fusion), kind=kCustom, calls=%fused_computation | custom fusion | bytes 2097168 | tf_op jit(solution)/shard_map/gather | solution.py:36
  155.0 4.1 %convolution_convert_fusion.3 = bf16[1024,512]{1,0:T(8,128)(2,1)} fusion(bf16[1024,1024]{1,0:T(8,128)(2,1)} %fusion.7, bf16[1024,512]{1,0:T(8,128)(2,1)} %bitcast.120), kind=kOutput, calls=%fused_computation.18 | convolution fusion | flops 1074266112 | bytes 4194304 | tf_op jit(solution)/shard_map/dot_general | solution.py:133
  159.1 6.5 %all-to-all-start.1 = ((bf16[8,128,512]{2,1,0:T(8,128)(2,1)}), bf16[8,128,512]{2,1,0:T(8,128)(2,1)}, u32[]{:S(2)}, u32[]{:S(2)}) async-start(bf16[8,128,512]{2,1,0:T(8,128)(2,1)} %bitcast.124), calls=%async_computation.1 | async-start | bytes 2097152 | tf_op jit(solution)/shard_map/all_to_all | solution.py:134
  165.6 4.2 %convolution_convert_fusion = bf16[1024,1024]{1,0:T(8,128)(2,1)} fusion(bf16[1024,512]{0,1:T(8,128)(2,1)} %all-gather.4.cloned.1.call-done, bf16[1024,512]{1,0:T(8,128)(2,1)} %bitcast.121), kind=kOutput, calls=%fused_computation.14 | convolution fusion | flops 1074790400 | bytes 4194304 | tf_op jit(solution)/shard_map/dot_general | solution.py:155
  169.7 11.3 %all-to-all-done.1 = bf16[8,128,512]{2,1,0:T(8,128)(2,1)} async-done(((bf16[8,128,512]{2,1,0:T(8,128)(2,1)}), bf16[8,128,512]{2,1,0:T(8,128)(2,1)}, u32[]{:S(2)}, u32[]{:S(2)}) %all-to-all-start.1) | async-done | bytes 1048608 | tf_op jit(solution)/shard_map/all_to_all | solution.py:134
  181.1 4.7 %all-to-all-start.2 = ((bf16[8,128,1024]{2,1,0:T(8,128)(2,1)}), bf16[8,128,1024]{2,1,0:T(8,128)(2,1)}, u32[]{:S(2)}, u32[]{:S(2)}) async-start(bf16[8,128,1024]{2,1,0:T(8,128)(2,1)} %bitcast.117), calls=%async_computation.2 | async-start | bytes 4194304 | tf_op jit(solution)/shard_map/all_to_all | solution.py:158
  185.8 1.4 reduce_sum.80
  187.1 0.1 copy.92
  187.3 3.0 %convolution_convert_fusion.2 = bf16[4,128,8,128]{3,1,2,0:T(8,128)(2,1)} fusion(bf16[128,4,128,1]{0,2,3,1:T(8,128)(2,1)S(1)} %bitcast.127, f32[4,8,128,128]{2,3,1,0:T(8,128)} %get-tuple-element.38, f32[4,8,128]{2,1,0:T(8,128)S(1)} %copy-done.9), kind=kOutput, calls=%fused_computation.17 | convolution fusion | flops 135790592 | bytes 3293184 | tf_op jit(solution)/shard_map/yxmd,dya->myxa/dot_general | solution.py:64
  190.3 2.3 %copy.105 = bf16[128,4096]{1,0:T(8,128)(2,1)} copy(bf16[128,4096]{0,1:T(8,128)(2,1)} %bitcast.126) | data formatting | bytes 2097152
  192.5 1.8 fusion.34
  194.3 5.4 %convolution_convert_fusion.1 = bf16[4,8,128,128]{2,3,1,0:T(8,128)(2,1)} fusion(bf16[128,4,128,1]{0,2,3,1:T(8,128)(2,1)S(1)} %copy.113, f32[4,128,128,8]{2,1,3,0:T(8,128)} %fusion.34, f32[4,8,128,128]{2,3,1,0:T(8,128)} %get-tuple-element.38, f32[4,8,128]{2,1,0:T(8,128)S(1)} %copy-done.9), kind=kOutput, calls=%fused_computation.16 | convolution fusion | flops 138416256 | bytes 5390336 | tf_op jit(solution)/shard_map/yxmd,dya->myxa/dot_general | solution.py:81
  199.7 2.4 %copy.106 = bf16[128,4096]{1,0:T(8,128)(2,1)} copy(bf16[128,4096]{0,1:T(8,128)(2,1)} %bitcast.125) | data formatting | bytes 2097152
  202.1 4.3 %fusion.9 = bf16[4,128,128]{1,2,0:T(8,128)(2,1)S(1)} fusion(bf16[128,4,8,128]{0,3,2,1:T(8,128)(2,1)S(1)} %bitcast.123, f32[4,128,128,8]{2,1,3,0:T(8,128)} %fusion.34, f32[4,8,128,128]{2,3,1,0:T(8,128)} %get-tuple-element.38, f32[4,8,128]{2,1,0:T(8,128)S(1)} %copy-done.9), kind=kOutput, calls=%fused_computation.21 | convolution fusion | flops 137957504 | bytes 5390336 | tf_op jit(solution)/shard_map/lbjm,jlbw->mlw/dot_general | solution.py:84
  206.4 0.8 copy.107
  207.1 5.1 %all-to-all-done.2 = bf16[8,128,1024]{2,1,0:T(8,128)(2,1)} async-done(((bf16[8,128,1024]{2,1,0:T(8,128)(2,1)}), bf16[8,128,1024]{2,1,0:T(8,128)(2,1)}, u32[]{:S(2)}, u32[]{:S(2)}) %all-to-all-start.2) | async-done | bytes 2097184 | tf_op jit(solution)/shard_map/all_to_all | solution.py:158
  212.2 3.1 %copy.129 = bf16[8,16,8,1024]{3,2,0,1:T(8,128)(2,1)} copy(bf16[8,16,8,1024]{3,2,1,0:T(8,128)(2,1)} %bitcast.55) | data formatting | bytes 4194304 | tf_op jit(solution)/shard_map/all_to_all | solution.py:158
  215.4 1.9 broadcast_multiply_fusion
  (31 shorter events, 0.2 us)
Async XLA Ops:
  7.2 78.7 %copy-start = (bf16[2048,512]{1,0:T(8,128)(2,1)S(1)}, bf16[2048,512]{1,0:T(8,128)(2,1)}, u32[]{:S(2)}) copy-start(bf16[2048,512]{1,0:T(8,128)(2,1)} %param.14) | copy-start | bytes 6291460
  11.4 5.4 %copy-start.5 = (s32[1,8]{1,0:T(1,128)S(1)}, s32[1,8]{1,0:T(1,128)}, u32[]{:S(2)}) copy-start(s32[1,8]{1,0:T(1,128)} %param.11) | copy-start | bytes 100
  11.4 5.4 %copy-start.6 = (s32[1,8]{1,0:T(1,128)S(1)}, s32[1,8]{1,0:T(1,128)}, u32[]{:S(2)}) copy-start(s32[1,8]{1,0:T(1,128)} %param.10) | copy-start | bytes 100
  11.4 5.4 %copy-start.7 = (s32[1,8]{1,0:T(1,128)S(1)}, s32[1,8]{1,0:T(1,128)}, u32[]{:S(2)}) copy-start(s32[1,8]{1,0:T(1,128)} %param.9) | copy-start | bytes 100
  11.4 36.0 %copy-start.3 = (bf16[128,512]{1,0:T(8,128)(2,1)S(1)}, bf16[128,512]{1,0:T(8,128)(2,1)}, u32[]{:S(2)}) copy-start(bf16[128,512]{1,0:T(8,128)(2,1)} %param.13) | copy-start | bytes 393220
  11.4 36.2 %copy-start.1 = (bf16[128,4096]{1,0:T(8,128)(2,1)S(1)}, bf16[128,4096]{1,0:T(8,128)(2,1)}, u32[]{:S(2)}) copy-start(bf16[128,4096]{1,0:T(8,128)(2,1)} %param.12) | copy-start | bytes 3145732
  11.4 45.8 %all-to-all-start = ((bf16[128,8,1024]{0,2,1:T(8,128)(2,1)}), bf16[128,8,1024]{0,2,1:T(8,128)(2,1)}, u32[]{:S(2)}, u32[]{:S(2)}) async-start(bf16[128,8,1024]{0,2,1:T(8,128)(2,1)} %bitcast.114), calls=%async_computation | async-start | bytes 4194304 | tf_op jit(solution)/shard_map/all_to_all | solution.py:124
  16.7 64.6 %all-gather.4.cloned.1.call-start = ((), (), s32[]{:S(2)}) async-start(), calls=%async_computation.4 | async-start | bytes 1179648 | tf_op jit(solution)/shard_map/all_gather | solution.py:145
  47.5 1.6 copy-start.4
  52.4 4.3 %copy-start.8 = (f32[4,8,128]{2,1,0:T(8,128)}, f32[4,8,128]{2,1,0:T(8,128)S(1)}, u32[]{:S(2)}) copy-start(f32[4,8,128]{2,1,0:T(8,128)S(1)} %get-tuple-element.37) | copy-start | bytes 49156
  56.8 158.6 %reduce-scatter.2.cloned.1.call-start = ((), (), s32[]{:S(2)}) async-start(), calls=%async_computation.5 | async-start | bytes 2621440 | tf_op jit(solution)/shard_map/reduce_scatter | solution.py:146
  85.9 0.7 collective-permute-start
  86.6 33.5 %collective-permute-start.1 = (bf16[256,512]{1,0:T(8,128)(2,1)S(1)}, bf16[256,512]{1,0:T(8,128)(2,1)}, u32[]{:S(2)}, u32[]{:S(2)}) collective-permute-start(bf16[256,512]{1,0:T(8,128)(2,1)S(1)} %collective-permute-done), channel_id=1, source_target_pairs={{0,1},{1,2},{2,3},{3,0},{4,5},{5,6},{6,7},{7,4},{8,9},{9,10},{10,1... | collective-permute-start | bytes 786440 | tf_op jit(solution)/shard_map/ppermute | solution.py:27
  103.2 44.8 %collective-permute-start.3 = (bf16[256,512]{1,0:T(8,128)(2,1)S(1)}, bf16[256,512]{1,0:T(8,128)(2,1)}, u32[]{:S(2)}, u32[]{:S(2)}) collective-permute-start(bf16[256,512]{1,0:T(8,128)(2,1)S(1)} %collective-permute-done), channel_id=1, source_target_pairs={{1,0},{2,1},{3,2},{0,3},{5,4},{6,5},{7,6},{4,7},{9,8},{10,9},{11,1... | collective-permute-start | bytes 786440 | tf_op jit(solution)/shard_map/ppermute | solution.py:30
  120.1 29.9 %collective-permute-start.2 = (bf16[256,512]{1,0:T(8,128)(2,1)}, bf16[256,512]{1,0:T(8,128)(2,1)}, u32[]{:S(2)}, u32[]{:S(2)}) collective-permute-start(bf16[256,512]{1,0:T(8,128)(2,1)} %collective-permute-done.1), channel_id=1, source_target_pairs={{0,1},{1,2},{2,3},{3,0},{4,5},{5,6},{6,7},{7,4},{8,9},{9,10},{10,1... | collective-permute-start | bytes 786440 | tf_op jit(solution)/shard_map/ppermute | solution.py:27
  159.1 22.0 %all-to-all-start.1 = ((bf16[8,128,512]{2,1,0:T(8,128)(2,1)}), bf16[8,128,512]{2,1,0:T(8,128)(2,1)}, u32[]{:S(2)}, u32[]{:S(2)}) async-start(bf16[8,128,512]{2,1,0:T(8,128)(2,1)} %bitcast.124), calls=%async_computation.1 | async-start | bytes 2097152 | tf_op jit(solution)/shard_map/all_to_all | solution.py:134
  181.1 6.2 %copy-start.9 = (f32[4,8,128]{2,1,0:T(8,128)S(1)}, f32[4,8,128]{2,1,0:T(8,128)}, u32[]{:S(2)}) copy-start(f32[4,8,128]{2,1,0:T(8,128)} %copy-done.8) | copy-start | bytes 49156
  181.1 31.1 %all-to-all-start.2 = ((bf16[8,128,1024]{2,1,0:T(8,128)(2,1)}), bf16[8,128,1024]{2,1,0:T(8,128)(2,1)}, u32[]{:S(2)}, u32[]{:S(2)}) async-start(bf16[8,128,1024]{2,1,0:T(8,128)(2,1)} %bitcast.117), calls=%async_computation.2 | async-start | bytes 4194304 | tf_op jit(solution)/shard_map/all_to_all | solution.py:158
  199.7 2.4 %copy-start.2 = (bf16[128,4096]{0,1:T(8,128)(2,1)S(1)}, bf16[128,4096]{0,1:T(8,128)(2,1)}, u32[]{:S(2)}) copy-start(bf16[128,4096]{0,1:T(8,128)(2,1)} %copy.127) | copy-start | bytes 3145732
Sparse Core Ops, SparseCore 0:
  56.9 24.3 all-gather.3
  85.9 66.3 reduce-scatter.1
